TPU v7x, 32 devices: a whole 2x2x4 slice. The times are simulated.
32 devices in a mesh: groups: 2 (over x), dp: 8 (over z, y), tensor: 2 (over core).
Axes of the slice: x: 2, y: 2, z: 4, core: 2. Of those that a mesh axis runs over, the one named last changes fastest.
Arguments:
- hidden_states: bfloat16 [3584, 5120], P(('groups', 'dp'), 'tensor'), parts along dimension 0, may hold values from -6 to 6
- input_gain: float32 [5120], replicated, may hold values from 0.1 to 1.9
- q_weight: bfloat16 [5120, 512], P(None, 'tensor'), may hold values from -0.078125 to 0.078125
- k_weight: bfloat16 [5120, 256], P(None, 'tensor'), may hold values from -0.078125 to 0.078125
- v_weight: bfloat16 [5120, 256], P(None, 'tensor'), may hold values from -0.078125 to 0.078125
- o_weight: bfloat16 [512, 5120], P('tensor'), may hold values from -0.25 to 0.25
- q_gain: float32 [128], replicated, may hold values from 0.6 to 13
- k_gain: float32 [128], replicated, may hold values from 0.6 to 13
- seq_lens: int32 [16, 5], P('groups'), parts along dimension 0, may hold values from 1 to 160, as said below
- dest: int32 [16, 5], P('groups'), parts along dimension 0, may hold values from 0 to 7, as said below
Outputs:
- mixed: bfloat16 [2560, 5120], P(('groups', 'dp'), 'tensor'), parts along dimension 0
There are 2 independent parts, one for each index of `groups`. A program takes and returns all parts, laid end to end along the dimension named above; an argument that names none is the same for every part. Nothing has to cross between parts.
Inputs may be any that keep to these rules, and one draw needn't show every extreme that they name: `seq_lens`: each replica's sequences lie packed from row 0 of its block in slot order. `dest`: slot 0 never moves. A replica either sends sequences or receives them, never both. At most 16 tokens in all go from one replica to any one other, and at most 160 tokens are processed by one replica; both bounds are reached.
All inputs are finite; a program needn't handle non-finite values.
Results may differ from a plain program's by a relative error of at most 0.004.
The roundings to bfloat16 on the way count: a program that leaves them out, or rounds other values in their place, can miss the bound.
Values may be sent and summed in bfloat16 or wider, within the bound.
A program may use at most 128 MiB of HBM per device.

v0:
```python
import jax
import jax.numpy as jnp
from jax import lax
from jax.sharding import PartitionSpec as P

HD = 128
CAPP = 16
LONG = 160
SHORT = 8
EPSILON = 1e-06
ROPE_BASE = 1000000.0
MASKED_SCORE = -1e30


def rms_scale(entries, gain):
    mean_square = jnp.mean(entries * entries, axis=-1, keepdims=True)
    return entries * lax.rsqrt(mean_square + EPSILON) * gain


def rotation(positions, width):
    half_head = width // 2
    frequency = ROPE_BASE ** (-2.0 * jnp.arange(half_head, dtype=jnp.float32) / width)
    angles = positions.astype(jnp.float32)[:, None] * frequency[None, :]
    return (jnp.cos(angles), jnp.sin(angles))


def rotate(entries, cosine, sine_part):
    half_head = entries.shape[-1] // 2
    first_half = entries[..., :half_head]
    second_half = entries[..., half_head:]
    return jnp.concatenate(
        [
            first_half * cosine - second_half * sine_part,
            second_half * cosine + first_half * sine_part,
        ],
        axis=-1,
    )


def sequence_table(seq_lens, dest):
    replicas, slots = seq_lens.shape
    lengths = seq_lens.reshape(-1)
    offsets = (jnp.cumsum(seq_lens, axis=1) - seq_lens).reshape(-1)
    source = jnp.broadcast_to(
        jnp.arange(replicas, dtype=jnp.int32)[:, None], (replicas, slots)
    ).reshape(-1)
    slot_index = jnp.broadcast_to(
        jnp.arange(slots, dtype=jnp.int32)[None, :], (replicas, slots)
    ).reshape(-1)
    target = dest.reshape(-1)
    order_key = (source - target) % replicas * slots + slot_index
    earlier = (target[None, :] == target[:, None]) & (order_key[None, :] < order_key[:, None])
    begins = jnp.sum(jnp.where(earlier, lengths[None, :], 0), axis=1)
    return (source, slot_index, lengths, target, offsets, begins)


def widen(half_rows):
    return lax.all_gather(half_rows, "tensor", axis=1, tiled=True)


def project(full_rows, positions, input_gain, q_weight, k_weight, v_weight, q_gain, k_gain):
    row_count = full_rows.shape[0]
    normed = rms_scale(full_rows.astype(jnp.float32), input_gain).astype(jnp.bfloat16)
    cosine, sine_part = rotation(positions, HD)
    queries = jnp.dot(normed, q_weight, preferred_element_type=jnp.float32).reshape(
        row_count, -1, HD
    )
    queries = rotate(rms_scale(queries, q_gain), cosine[:, None, :], sine_part[:, None, :]).astype(
        jnp.bfloat16
    )
    key_rows = jnp.dot(normed, k_weight, preferred_element_type=jnp.float32)
    key_rows = rotate(rms_scale(key_rows, k_gain), cosine, sine_part).astype(jnp.bfloat16)
    value_rows = jnp.dot(normed, v_weight, preferred_element_type=jnp.float32).astype(jnp.bfloat16)
    return (queries, key_rows, value_rows)


def attend(queries, key_rows, value_rows, segment, position):
    scores = jnp.einsum(
        "qhd,kd->hqk", queries, key_rows, preferred_element_type=jnp.float32
    ) * queries.shape[-1] ** (-0.5)
    allowed = (segment[:, None] == segment[None, :]) & (position[None, :] <= position[:, None])
    scores = jnp.where(allowed[None], scores, MASKED_SCORE)
    row_max = jnp.max(scores, axis=2, keepdims=True)
    exp_scores = jnp.exp(scores - row_max)
    weights = (exp_scores / jnp.sum(exp_scores, axis=2, keepdims=True)).astype(jnp.bfloat16)
    return jnp.einsum("hqk,kd->qhd", weights, value_rows, preferred_element_type=jnp.float32)


def per_device(
    hidden_states,
    input_gain,
    q_weight,
    k_weight,
    v_weight,
    o_weight,
    q_gain,
    k_gain,
    seq_lens,
    dest,
):
    replicas = lax.axis_size("dp")
    replica = lax.axis_index("dp")
    tensor_part = lax.axis_index("tensor")
    home_rows, half_width = hidden_states.shape
    slots = seq_lens.shape[1]
    work_rows = max(LONG, slots * SHORT + (slots - 1) * CAPP)
    source, slot_index, lengths, target, offsets, begins = sequence_table(seq_lens, dest)
    seq_ident = jnp.arange(lengths.shape[0], dtype=jnp.int32)
    shipped_seq = source != target
    pair_earlier = (
        (source[None, :] == source[:, None])
        & (target[None, :] == target[:, None])
        & (slot_index[None, :] < slot_index[:, None])
    )
    send_begin = jnp.sum(jnp.where(pair_earlier, lengths[None, :], 0), axis=1)
    peer_ids = jnp.arange(replicas, dtype=jnp.int32)[:, None, None]
    slot_rows = jnp.arange(CAPP, dtype=jnp.int32)[None, :, None]
    inside = (send_begin <= slot_rows) & (slot_rows < send_begin + lengths)
    outgoing = inside & shipped_seq & (source == replica) & (target == peer_ids)
    send_rows = jnp.sum(jnp.where(outgoing, offsets + slot_rows - send_begin, 0), axis=2).reshape(
        -1
    )
    incoming = inside & shipped_seq & (target == replica) & (source == peer_ids)
    arrive_live = jnp.any(incoming, axis=2)
    arrive_seg = jnp.where(arrive_live, jnp.sum(jnp.where(incoming, seq_ident, 0), axis=2), -1)
    arrive_pos = jnp.sum(jnp.where(incoming, slot_rows - send_begin, 0), axis=2)
    home_ids = jnp.arange(home_rows, dtype=jnp.int32)[:, None]
    resident = (source == replica) & (offsets <= home_ids) & (home_ids < offsets + lengths)
    home_live = jnp.any(resident, axis=1)
    home_seg = jnp.where(home_live, jnp.sum(jnp.where(resident, seq_ident, 0), axis=1), -1)
    home_pos = jnp.sum(jnp.where(resident, home_ids - offsets, 0), axis=1)
    work_ids = jnp.arange(work_rows, dtype=jnp.int32)[:, None]
    placed = (target == replica) & (begins <= work_ids) & (work_ids < begins + lengths)
    work_live = jnp.any(placed, axis=1)
    work_pos = jnp.sum(jnp.where(placed, work_ids - begins, 0), axis=1)
    pool_base = jnp.where(source == replica, offsets, home_rows + source * CAPP + send_begin)
    pool_row = jnp.sum(jnp.where(placed, pool_base, 0), axis=1) + work_pos
    home_full = widen(hidden_states)
    outbound = jnp.take(home_full, send_rows, axis=0).reshape(replicas, CAPP, -1)
    arrived = lax.all_to_all(outbound, "dp", split_axis=0, concat_axis=0, tiled=True)
    pool_full = jnp.concatenate([home_full, arrived.reshape(replicas * CAPP, -1)], axis=0)
    pool_half = lax.dynamic_slice_in_dim(pool_full, tensor_part * half_width, half_width, 1)
    pool_pos = jnp.concatenate([home_pos, arrive_pos.reshape(-1)], axis=0)
    queries, key_rows, value_rows = project(
        pool_full, pool_pos, input_gain, q_weight, k_weight, v_weight, q_gain, k_gain
    )
    home_out = attend(
        queries[:home_rows], key_rows[:home_rows], value_rows[:home_rows], home_seg, home_pos
    )
    arrive_out = jax.vmap(attend)(
        queries[home_rows:].reshape(replicas, CAPP, -1, HD),
        key_rows[home_rows:].reshape(replicas, CAPP, HD),
        value_rows[home_rows:].reshape(replicas, CAPP, HD),
        arrive_seg,
        arrive_pos,
    )
    head_out = jnp.concatenate([home_out, arrive_out.reshape(replicas * CAPP, -1, HD)], axis=0)
    head_out = head_out.reshape(home_rows + replicas * CAPP, -1).astype(jnp.bfloat16)
    all_heads = lax.all_gather(head_out, "tensor", axis=1, tiled=True)
    own_columns = lax.all_to_all(o_weight, "tensor", split_axis=1, concat_axis=0, tiled=True)
    summed = jnp.dot(all_heads, own_columns, preferred_element_type=jnp.float32)
    mixed_pool = pool_half.astype(jnp.float32) + summed
    mixed = jnp.where(work_live[:, None], jnp.take(mixed_pool, pool_row, axis=0), 0.0)
    return mixed.astype(jnp.bfloat16)


def solution(mesh):
    return jax.shard_map(
        per_device,
        mesh=mesh,
        in_specs=(
            P(("groups", "dp"), "tensor"),
            P(),
            P(None, "tensor"),
            P(None, "tensor"),
            P(None, "tensor"),
            P("tensor", None),
            P(),
            P(),
            P("groups", None),
            P("groups", None),
        ),
        out_specs=P(("groups", "dp"), "tensor"),
        check_vma=False,
    )
```

profile of v0, /device:TPU:0, one launch (start us, length us, event | category | flops | bytes accessed | tf_op | source)
XLA Modules:
  0.0 107.7 jit_solution(4255287312289752939)
XLA Ops:
  6.5 0.0 copy-start
  6.5 0.0 all-gather.2.cloned.1.call-start
  6.5 0.7 all-gather.2.cloned.1.call-update
  7.3 4.5 %copy.54 = bf16[256,5120]{0,1:T(8,128)(2,1)} copy(bf16[256,5120]{1,0:T(8,128)(2,1)} %param.15) | data formatting | bytes 5242880 | tf_op args[5]
  11.7 5.1 %all-to-all-start.1 = ((bf16[256,2,2560]{0,2,1:T(8,128)(2,1)}), bf16[256,2,2560]{0,2,1:T(8,128)(2,1)}, u32[]{:S(2)}, u32[]{:S(2)}) async-start(bf16[256,2,2560]{0,2,1:T(8,128)(2,1)} %bitcast.82), calls=%async_computation.1 | async-start | bytes 5242880 | tf_op jit(solution)/shard_map/all_to_all | solution.py:160
  16.9 0.1 reshape.679
  17.0 0.0 copy-done.6
  17.0 0.1 reshape.678
  17.0 0.1 reshape.680
  17.1 0.0 copy-done.4
  17.1 0.1 broadcast_in_dim.197
  17.2 0.2 reduce_window_sum.11
  17.4 0.1 reshape.681
  17.5 0.2 select_reduce_fusion.6
  17.7 0.2 select_reduce_fusion
  18.0 0.1 reshape.682
  18.1 4.4 %all-gather.2.cloned.1.call-done = bf16[224,5120]{1,0:T(8,128)(2,1)} async-done(((bf16[224,2560]{1,0:T(8,128)(2,1)}), bf16[224,5120]{1,0:T(8,128)(2,1)}) %all-gather.2.cloned.1.call-update) | async-done | bytes 2293776 | tf_op jit(solution)/shard_map/all_gather | solution.py:58
  22.5 5.6 %gather_fusion = bf16[128,5120]{1,0:T(8,128)(2,1)} fusion(bf16[224,5120]{1,0:T(8,128)(2,1)} %all-gather.2.cloned.1.call-done, s32[1024]{0:T(1024)S(1)} %pad_clamp_fusion.1), kind=kCustom, calls=%fused_computation | custom fusion | bytes 2621952 | tf_op jit(solution)/shard_map/jit(_take)/gather | solution.py:139
  28.1 2.6 %broadcast_select_fusion = bf16[8,16,5120]{2,1,0:T(8,128)(2,1)} fusion(bf16[8,16,5120]{2,1,0:T(8,128)(2,1)} %bitcast.83, pred[8,16]{1,0:T(8,128)(4,1)S(1)} %compare_and_fusion.4), kind=kLoop, calls=%fused_computation.15 | loop fusion | flops 655360 | bytes 2621568 | tf_op jit(solution)/shard_map/jit(_take)/select_n | solution.py:139
  30.7 0.0 all-to-all-done.1
  30.7 6.5 %all-to-all-start = ((bf16[8,16,5120]{2,1,0:T(8,128)(2,1)}), bf16[8,16,5120]{2,1,0:T(8,128)(2,1)}, u32[]{:S(2)}, u32[]{:S(2)}) async-start(bf16[8,16,5120]{2,1,0:T(8,128)(2,1)} %broadcast_select_fusion), calls=%async_computation | async-start | bytes 2621440 | tf_op jit(solution)/shard_map/all_to_all | solution.py:140
  37.2 0.3 fusion.20
  37.6 0.1 concatenate.30
  37.6 4.4 %copy.55 = bf16[2,256,2560]{2,1,0:T(8,128)(2,1)} copy(bf16[2,256,2560]{1,2,0:T(8,128)(2,1)} %bitcast.17) | data formatting | bytes 5242880 | tf_op jit(solution)/shard_map/all_to_all | solution.py:160
  42.0 0.5 multiply_power_fusion
  42.6 0.1 select_reduce_fusion.2
  42.7 0.1 add_convert_fusion.2
  42.8 0.1 select_reduce_fusion.3
  42.9 0.2 and_reduce_fusion
  43.1 0.1 fusion.59
  43.2 0.1 fusion.58
  43.4 0.1 compare_and_fusion.1
  43.5 0.8 compare_and_fusion
  44.2 24.8 %all-to-all-done = bf16[8,16,5120]{2,1,0:T(8,128)(2,1)} async-done(((bf16[8,16,5120]{2,1,0:T(8,128)(2,1)}), bf16[8,16,5120]{2,1,0:T(8,128)(2,1)}, u32[]{:S(2)}, u32[]{:S(2)}) %all-to-all-start) | async-done | bytes 1310752 | tf_op jit(solution)/shard_map/all_to_all | solution.py:140
  69.1 3.0 %fusion.2 = f32[352]{0:T(512)S(1)} fusion(bf16[128,5120]{1,0:T(8,128)(2,1)} %bitcast.2, bf16[224,5120]{1,0:T(8,128)(2,1)} %all-gather.2.cloned.1.call-done), kind=kLoop, calls=%fused_computation.6 | loop fusion | flops 10813088 | bytes 3605888 | tf_op jit(solution)/shard_map/reduce_sum | solution.py:16
  72.1 2.1 %fusion.4 = bf16[352,5120]{1,0:T(8,128)(2,1)S(1)} fusion(f32[5120]{0:T(1024)S(1)} %copy-done.5, f32[352]{0:T(512)S(1)} %add_rsqrt_fusion.2, bf16[128,5120]{1,0:T(8,128)(2,1)} %bitcast.2, bf16[224,5120]{1,0:T(8,128)(2,1)S(1)} %copy-done.1), kind=kLoop, calls=%fused_computation.8 | loop fusion | flops 12615680 | bytes 7230848 | tf_op jit(solution)/shard_map/convert_element_type | solution.py:63
  74.2 0.0 copy-start.2
  74.2 1.8 %copy-done.2 = bf16[352,5120]{1,0:T(8,128)(2,1)} copy-done((bf16[352,5120]{1,0:T(8,128)(2,1)}, bf16[352,5120]{1,0:T(8,128)(2,1)S(1)}, u32[]{:S(2)}) %copy-start.2) | copy-done | bytes 3604504
  76.0 1.1 %fusion.68 = f32[352,256]{1,0:T(8,128)S(1)} fusion(bf16[352,5120]{1,0:T(8,128)(2,1)S(1)} %fusion.4, bf16[5120,256]{1,0:T(8,128)(2,1)S(1)} %copy-done), kind=kOutput, calls=%fused_computation.131 | convolution fusion | flops 922746880 | bytes 6586368 | tf_op jit(solution)/shard_map/dot_general | solution.py:65
  77.2 0.2 reshape.684
  77.4 0.4 multiply_reduce_fusion
  77.8 0.1 copy.47
  77.9 0.0 copy-start.7
  77.9 0.0 copy-start.8
  77.9 3.6 %multiply_reduce_fusion.1 = (f32[352]{0:T(512)S(1)}, f32[352,128]{1,0:T(8,128)S(1)}) fusion(bf16[352,5120]{1,0:T(8,128)(2,1)} %copy-done.2, bf16[5120,128]{1,0:T(8,128)(2,1)} %param.13), kind=kOutput, calls=%fused_computation.46 | convolution fusion | flops 461463200 | bytes 5096832 | tf_op jit(solution)/shard_map/dot_general | solution.py:71
  81.6 0.2 fusion.16
  81.8 0.1 multiply_multiply_fusion
  81.9 0.0 copy-done.9
  81.9 0.8 multiply_cosine_fusion
  82.7 0.2 subtract_convert_fusion
  82.9 0.1 pad_maximum_fusion.2
  83.0 0.1 pad_maximum_fusion.3
  83.0 0.3 fusion.13
  83.3 0.3 fusion.60
  83.6 0.0 copy-done.3
  83.6 1.2 %fusion.63 = (f32[2,224]{1,0:T(2,128)S(1)}, f32[2,224,224]{1,2,0:T(8,128)}) fusion(pred[224,224]{0,1:T(8,128)(4,1)S(1)} %copy-done.3, bf16[352,2,64]{2,0,1:T(8,128)(2,1)S(1)} %get-tuple-element.15, bf16[352,2,64]{2,0,1:T(8,128)(2,1)S(1)} %get-tuple-element.16, bf16[352,64]{1,0:T(8,128)(2,1)S(1)} %get-tuple-element.22, ...), kind=kOutput, calls=%fused_computation.130 | convolution fusion | flops 26435808 | bytes 723712 | tf_op jit(solution)/shard_map/sub | solution.py:84
  84.8 3.5 %convolution_convert_fusion.1 = bf16[352,128]{1,0:T(8,128)(2,1)S(1)} fusion(bf16[352,5120]{1,0:T(8,128)(2,1)} %copy-done.2, bf16[5120,128]{1,0:T(8,128)(2,1)} %param.14), kind=kOutput, calls=%fused_computation.23 | convolution fusion | flops 461418496 | bytes 5005312 | tf_op jit(solution)/shard_map/dot_general | solution.py:73
  88.4 0.3 fusion.14
  88.7 0.2 fusion.15
  88.9 0.1 copy.53
  89.0 2.2 %all_gather.7 = bf16[352,512]{1,0:T(8,128)(2,1)S(1)} all-gather(bf16[352,256]{1,0:T(8,128)(2,1)S(1)} %pad_maximum_fusion.1), channel_id=1, replica_groups=mesh['groups'=2,'dp'=8,'tensor'=2] {'tensor'}, dimensions={1}, use_global_device_ids=true | all-gather | bytes 540672 | tf_op jit(solution)/shard_map/all_gather | solution.py:159
  91.3 4.5 %convolution_add_fusion = bf16[352,2560]{1,0:T(8,128)(2,1)} fusion(bf16[352,512]{1,0:T(8,128)(2,1)S(1)} %all_gather.7, bf16[512,2560]{1,0:T(8,128)(2,1)} %bitcast.84, s32[]{:T(128)S(6)} %select_n.145, bf16[224,5120]{1,0:T(8,128)(2,1)} %all-gather.2.cloned.1.call-done, bf16[128,5120]{1,0:T(8,128)(2,1)} %bitcast.2), kind=kOutput, calls=%fused_computation.9 | convolution fusion | flops 928153600 | bytes 8388612 | tf_op jit(solution)/shard_map/dot_general | solution.py:161
  95.8 3.6 %gather_fusion.1 = bf16[160,2560]{1,0:T(8,128)(2,1)S(1)} fusion(bf16[352,2560]{1,0:T(8,128)(2,1)} %convolution_add_fusion, s32[1024]{0:T(1024)S(1)} %pad_clamp_fusion), kind=kCustom, calls=%fused_computation.1 | custom fusion | bytes 1639040 | tf_op jit(solution)/shard_map/jit(_take)/gather | solution.py:163
  99.5 1.3 %select_convert_fusion = bf16[160,2560]{1,0:T(8,128)(2,1)} fusion(bf16[160,2560]{1,0:T(8,128)(2,1)S(1)} %gather_fusion.1, pred[160]{0:T(512)(128)(4,1)S(1)} %get-tuple-element.13, pred[160]{0:T(512)(128)(4,1)S(1)} %fusion.58), kind=kLoop, calls=%fused_computation.14 | loop fusion | flops 819200 | bytes 1638720 | tf_op jit(solution)/shard_map/convert_element_type | solution.py:164
  (38 shorter events, 0.2 us)
Async XLA Ops:
  6.5 69.5 %copy-start = (bf16[5120,256]{1,0:T(8,128)(2,1)S(1)}, bf16[5120,256]{1,0:T(8,128)(2,1)}, u32[]{:S(2)}) copy-start(bf16[5120,256]{1,0:T(8,128)(2,1)} %param.12) | copy-start | bytes 7864324
  6.5 16.0 %all-gather.2.cloned.1.call-start = ((), (), s32[]{:S(2)}) async-start(), calls=%async_computation.2 | async-start | bytes 3440640 | tf_op jit(solution)/shard_map/all_gather | solution.py:58
  11.7 5.3 %copy-start.6 = (s32[8,5]{1,0:T(8,128)S(1)}, s32[8,5]{1,0:T(8,128)}, u32[]{:S(2)}) copy-start(s32[8,5]{1,0:T(8,128)} %param.19) | copy-start | bytes 484
  11.7 5.4 %copy-start.4 = (s32[8,5]{1,0:T(8,128)S(1)}, s32[8,5]{1,0:T(8,128)}, u32[]{:S(2)}) copy-start(s32[8,5]{1,0:T(8,128)} %param.18) | copy-start | bytes 484
  11.7 19.0 %all-to-all-start.1 = ((bf16[256,2,2560]{0,2,1:T(8,128)(2,1)}), bf16[256,2,2560]{0,2,1:T(8,128)(2,1)}, u32[]{:S(2)}, u32[]{:S(2)}) async-start(bf16[256,2,2560]{0,2,1:T(8,128)(2,1)} %bitcast.82), calls=%async_computation.1 | async-start | bytes 5242880 | tf_op jit(solution)/shard_map/all_to_all | solution.py:160
  30.7 38.3 %all-to-all-start = ((bf16[8,16,5120]{2,1,0:T(8,128)(2,1)}), bf16[8,16,5120]{2,1,0:T(8,128)(2,1)}, u32[]{:S(2)}, u32[]{:S(2)}) async-start(bf16[8,16,5120]{2,1,0:T(8,128)(2,1)} %broadcast_select_fusion), calls=%async_computation | async-start | bytes 2621440 | tf_op jit(solution)/shard_map/all_to_all | solution.py:140
  42.0 30.0 %copy-start.5 = (f32[5120]{0:T(1024)S(1)}, f32[5120]{0:T(1024)}, u32[]{:S(2)}) copy-start(f32[5120]{0:T(1024)} %param.11) | copy-start | bytes 61444
  69.1 3.0 %copy-start.1 = (bf16[224,5120]{1,0:T(8,128)(2,1)S(1)}, bf16[224,5120]{1,0:T(8,128)(2,1)}, u32[]{:S(2)}) copy-start(bf16[224,5120]{1,0:T(8,128)(2,1)} %all-gather.2.cloned.1.call-done) | copy-start | bytes 6881284
  74.2 1.8 %copy-start.2 = (bf16[352,5120]{1,0:T(8,128)(2,1)}, bf16[352,5120]{1,0:T(8,128)(2,1)S(1)}, u32[]{:S(2)}) copy-start(bf16[352,5120]{1,0:T(8,128)(2,1)S(1)} %fusion.4) | copy-start | bytes 10813444
  77.9 3.7 %copy-start.7 = (f32[128]{0:T(128)S(1)}, f32[128]{0:T(128)}, u32[]{:S(2)}) copy-start(f32[128]{0:T(128)} %param.16) | copy-start | bytes 1540
  77.9 3.8 %copy-start.8 = (f32[128]{0:T(128)S(1)}, f32[128]{0:T(128)}, u32[]{:S(2)}) copy-start(f32[128]{0:T(128)} %param.17) | copy-start | bytes 1540
  77.9 3.9 %copy-start.9 = (f32[64]{0:T(128)S(1)}, f32[64]{0:T(128)}, u32[]{:S(2)}) copy-start(f32[64]{0:T(128)} %multiply_power_fusion) | copy-start | bytes 772
  81.5 2.1 %copy-start.3 = (pred[224,224]{0,1:T(8,128)(4,1)S(1)}, pred[224,224]{0,1:T(8,128)(4,1)}, u32[]{:S(2)}) copy-start(pred[224,224]{0,1:T(8,128)(4,1)} %compare_and_fusion) | copy-start | bytes 150532
  84.8 3.6 %copy-start.10 = (f32[2,224,224]{1,2,0:T(8,128)S(1)}, f32[2,224,224]{1,2,0:T(8,128)}, u32[]{:S(2)}) copy-start(f32[2,224,224]{1,2,0:T(8,128)} %get-tuple-element.37) | copy-start | bytes 1204228
Sparse Core Ops, SparseCore 0:
  8.9 13.5 all-gather.1
where the time goes:
time: 108 us
  waiting for transfers between devices  30 us (28%)
  local copies, waits for them, and re-layouts  20.9 us (19%)
  matrix products  15.1 us (14%)
  other arithmetic  14.1 us (13%)
  between operations  13.8 us (13%)
  starting transfers between devices  11.6 us (11%)
  blocking collectives  2.24 us (2%)
    all_to_all x1, waiting for transfers between devices, per_device(): lax.all_to_all(outbound, 'dp', split_axis=0, concat_axis=0, tiled=True)  24.8 us
    all_to_all x1, starting transfers between devices, per_device(): lax.all_to_all(outbound, 'dp', split_axis=0, concat_axis=0, tiled=True)  6.46 us
    unnamed x24, local copies, waits for them, and re-layouts  6.35 us
    gather x1, local copies, waits for them, and re-layouts, per_device(): jnp.take(home_full, send_rows, axis=0).reshape(replicas, CAPP, -1)  5.64 us
    all_to_all x1, starting transfers between devices, per_device(): lax.all_to_all(o_weight, 'tensor', split_axis=1, concat_axis=0, tiled=True)  5.14 us
    dot_general x1, matrix products, per_device(): summed = jnp.dot(all_heads, own_columns, preferred_element_type=jnp.float32)  4.54 us
    all_gather x1, waiting for transfers between devices, widen(): return lax.all_gather(half_rows, 'tensor', axis=1, tiled=True)  4.41 us
    all_to_all x1, local copies, waits for them, and re-layouts, per_device(): lax.all_to_all(o_weight, 'tensor', split_axis=1, concat_axis=0, tiled=True)  4.4 us
  transfers between devices with their start and end apart: 3, of which 2 were waited for; matrix products, arithmetic and copies ran while one was open for 19% of the time, Pallas kernels for 0%

commit v1 on v0

--- a/solution.py
+++ b/solution.py
@@ -157,7 +157,16 @@
     head_out = jnp.concatenate([home_out, arrive_out.reshape(replicas * CAPP, -1, HD)], axis=0)
     head_out = head_out.reshape(home_rows + replicas * CAPP, -1).astype(jnp.bfloat16)
     all_heads = lax.all_gather(head_out, "tensor", axis=1, tiled=True)
-    own_columns = lax.all_to_all(o_weight, "tensor", split_axis=1, concat_axis=0, tiled=True)
+
+    def manage_scales_now(content, net_axis, row_dim, array_dim):
+        return jnp.concatenate(
+            lax.all_to_all(
+                jnp.stack(jnp.split(content, lax.axis_size(net_axis), axis=row_dim)), net_axis, 0, 0
+            ),
+            array_dim,
+        )
+
+    own_columns = manage_scales_now(o_weight, "tensor", 1, 0)
     summed = jnp.dot(all_heads, own_columns, preferred_element_type=jnp.float32)
     mixed_pool = pool_half.astype(jnp.float32) + summed
     mixed = jnp.where(work_live[:, None], jnp.take(mixed_pool, pool_row, axis=0), 0.0)

time: 108 us -> 113 us (1.046)
  waiting for transfers between devices: 30 us -> 37.7 us
  local copies, waits for them, and re-layouts: 20.9 us -> 15.3 us
  other arithmetic: 14.1 us -> 17.2 us
    all_gather x1, waiting for transfers between devices: 4.41 us -> 10.2 us  [widen(): return lax.all_gather(half_rows, 'tensor', axis=1, tiled=True)]
    unnamed x24 -> x19, local copies, waits for them, and re-layouts: 6.35 us -> 1.82 us
    all_to_all x1 -> x0, local copies, waits for them, and re-layouts: 4.4 us -> none  [per_device(): lax.all_to_all(o_weight, 'tensor', split_axis=1, concat_axis=0, tiled=True)]
    all_to_all x1, waiting for transfers between devices: 24.8 us -> 26.8 us  [per_device(): lax.all_to_all(outbound, 'dp', split_axis=0, concat_axis=0, tiled=True)]
    another operation x0 -> x1, local copies, waits for them, and re-layouts: none -> 1.88 us  [manage_scales_now(): jnp.stack(jnp.split(content, lax.axis_size(net_axis), axis=row_dim))]
    another operation x1 -> x2, other arithmetic: 0.19 us -> 1.97 us  [the longest x1 1.78 us: manage_scales_now(): jnp.stack(jnp.split(content, lax.axis_size(net_axis), axis=row_dim))]
  transfers between devices with their start and end apart: 3 -> 3, of which waited for: 2 -> 2; matrix products, arithmetic and copies ran while one was open for 19% -> 25% of each run, Pallas kernels for 0% -> 0%
where the time goes in v1:
time: 113 us; the launch traced here: 112 us
  waiting for transfers between devices  37.7 us (33%)
  other arithmetic  17.2 us (15%)
  local copies, waits for them, and re-layouts  15.3 us (14%)
  matrix products  15.1 us (13%)
  between operations  13.8 us (12%)
  starting transfers between devices  10.8 us (10%)
  blocking collectives  2.35 us (2%)
    all_to_all x1, waiting for transfers between devices, per_device(): lax.all_to_all(outbound, 'dp', split_axis=0, concat_axis=0, tiled=True)  26.8 us
    all_gather x1, waiting for transfers between devices, widen(): return lax.all_gather(half_rows, 'tensor', axis=1, tiled=True)  10.2 us
    all_to_all x1, starting transfers between devices, per_device(): lax.all_to_all(outbound, 'dp', split_axis=0, concat_axis=0, tiled=True)  5.77 us
    gather x1, local copies, waits for them, and re-layouts, per_device(): jnp.take(home_full, send_rows, axis=0).reshape(replicas, CAPP, -1)  5.63 us
    all_to_all x1, starting transfers between devices, manage_scales_now(): lax.all_to_all(jnp.stack(jnp.split(content, lax.axis_size(net_axis), axis...  5.01 us
    dot_general x1, matrix products, per_device(): summed = jnp.dot(all_heads, own_columns, preferred_element_type=jnp.float32)  4.54 us
    gather x1, local copies, waits for them, and re-layouts, per_device(): jnp.take(mixed_pool, pool_row, axis=0)  3.63 us
    dot_general x1, matrix products, project(): key_rows = jnp.dot(normed, k_weight, preferred_element_type=jnp.float32)  3.6 us
  transfers between devices with their start and end apart: 3, of which 2 were waited for; matrix products, arithmetic and copies ran while one was open for 25% of the time, Pallas kernels for 0%

profile of v1, /device:TPU:0, one launch (start us, length us, event | category | flops | bytes accessed | tf_op | source)
XLA Modules:
  0.0 112.1 jit_solution(11339923883213322993)
XLA Ops:
  6.5 0.0 copy-start
  6.5 0.0 all-gather.2.cloned.1.call-start
  6.5 0.7 all-gather.2.cloned.1.call-update
  7.3 0.1 reshape.679
  7.4 0.8 reshape.678
  8.1 0.1 reshape.680
  8.2 0.8 broadcast_in_dim.197
  9.0 0.8 reduce_window_sum.11
  9.8 0.7 sub.80
  10.5 0.1 reshape.681
  10.6 0.2 select_reduce_fusion.6
  10.9 0.2 select_reduce_fusion
  11.1 0.1 reshape.682
  11.2 0.4 fusion.20
  11.5 0.1 concatenate.30
  11.6 0.1 select_reduce_fusion.2
  11.7 0.1 add_convert_fusion.2
  11.8 0.1 select_reduce_fusion.3
  12.0 0.2 and_reduce_fusion
  12.2 0.1 fusion.59
  12.3 10.2 %all-gather.2.cloned.1.call-done = bf16[224,5120]{1,0:T(8,128)(2,1)} async-done(((bf16[224,2560]{1,0:T(8,128)(2,1)}), bf16[224,5120]{1,0:T(8,128)(2,1)}) %all-gather.2.cloned.1.call-update) | async-done | bytes 2293776 | tf_op jit(solution)/shard_map/all_gather | solution.py:58
  22.5 5.6 %gather_fusion = bf16[128,5120]{1,0:T(8,128)(2,1)} fusion(bf16[224,5120]{1,0:T(8,128)(2,1)} %all-gather.2.cloned.1.call-done, s32[1024]{0:T(1024)S(1)} %pad_clamp_fusion.1), kind=kCustom, calls=%fused_computation | custom fusion | bytes 2621952 | tf_op jit(solution)/shard_map/jit(_take)/gather | solution.py:139
  28.1 2.6 %broadcast_select_fusion = bf16[8,16,5120]{2,1,0:T(8,128)(2,1)} fusion(bf16[8,16,5120]{2,1,0:T(8,128)(2,1)} %bitcast.84, pred[8,16]{1,0:T(8,128)(4,1)S(1)} %compare_and_fusion.4), kind=kLoop, calls=%fused_computation.18 | loop fusion | flops 655360 | bytes 2621568 | tf_op jit(solution)/shard_map/jit(_take)/select_n | solution.py:139
  30.7 5.8 %all-to-all-start = ((bf16[8,16,5120]{2,1,0:T(8,128)(2,1)}), bf16[8,16,5120]{2,1,0:T(8,128)(2,1)}, u32[]{:S(2)}, u32[]{:S(2)}) async-start(bf16[8,16,5120]{2,1,0:T(8,128)(2,1)} %broadcast_select_fusion), calls=%async_computation | async-start | bytes 2621440 | tf_op jit(solution)/shard_map/all_to_all | solution.py:140
  36.5 0.5 multiply_power_fusion
  37.0 0.1 fusion.58
  37.1 0.1 compare_and_fusion.1
  37.2 0.8 compare_and_fusion
  38.0 1.9 %slice_bitcast_fusion.1 = (bf16[1,256,2560]{2,1,0:T(8,128)(2,1)S(1)}, bf16[1,256,2560]{2,1,0:T(8,128)(2,1)S(1)}) fusion(bf16[256,5120]{1,0:T(8,128)(2,1)} %param.15), kind=kLoop, calls=%fused_computation.17 | loop fusion | bytes 5242880 | tf_op jit(solution)/shard_map/stack | solution.py:164
  39.9 1.8 %pad_maximum_fusion.1 = bf16[2,256,2560]{2,1,0:T(8,128)(2,1)} fusion(bf16[1,256,2560]{2,1,0:T(8,128)(2,1)S(1)} %get-tuple-element.16, bf16[1,256,2560]{2,1,0:T(8,128)(2,1)S(1)} %get-tuple-element.15), kind=kLoop, calls=%fused_computation.13 | loop fusion | flops 1310720 | bytes 5242880 | tf_op jit(solution)/shard_map/stack | solution.py:164
  41.7 26.8 %all-to-all-done = bf16[8,16,5120]{2,1,0:T(8,128)(2,1)} async-done(((bf16[8,16,5120]{2,1,0:T(8,128)(2,1)}), bf16[8,16,5120]{2,1,0:T(8,128)(2,1)}, u32[]{:S(2)}, u32[]{:S(2)}) %all-to-all-start) | async-done | bytes 1310752 | tf_op jit(solution)/shard_map/all_to_all | solution.py:140
  68.4 5.0 %all-to-all-start.1 = ((bf16[2,256,2560]{2,1,0:T(8,128)(2,1)}), bf16[2,256,2560]{2,1,0:T(8,128)(2,1)}, u32[]{:S(2)}, u32[]{:S(2)}) async-start(bf16[2,256,2560]{2,1,0:T(8,128)(2,1)} %pad_maximum_fusion.1), calls=%async_computation.1 | async-start | bytes 5242880 | tf_op jit(solution)/shard_map/all_to_all | solution.py:163
  73.4 0.0 copy-start.1
  73.5 0.0 copy-start.4
  73.5 3.0 %fusion.2 = f32[352]{0:T(512)S(1)} fusion(bf16[128,5120]{1,0:T(8,128)(2,1)} %bitcast.2, bf16[224,5120]{1,0:T(8,128)(2,1)} %all-gather.2.cloned.1.call-done), kind=kLoop, calls=%fused_computation.6 | loop fusion | flops 10813088 | bytes 3605888 | tf_op jit(solution)/shard_map/reduce_sum | solution.py:16
  76.5 0.0 copy-done.1
  76.5 2.1 %fusion.4 = bf16[352,5120]{1,0:T(8,128)(2,1)S(1)} fusion(f32[5120]{0:T(1024)S(1)} %copy-done.4, f32[352]{0:T(512)S(1)} %add_rsqrt_fusion.2, bf16[128,5120]{1,0:T(8,128)(2,1)} %bitcast.2, bf16[224,5120]{1,0:T(8,128)(2,1)S(1)} %copy-done.1), kind=kLoop, calls=%fused_computation.8 | loop fusion | flops 12615680 | bytes 7230848 | tf_op jit(solution)/shard_map/convert_element_type | solution.py:63
  78.6 1.8 %copy-done.2 = bf16[352,5120]{1,0:T(8,128)(2,1)} copy-done((bf16[352,5120]{1,0:T(8,128)(2,1)}, bf16[352,5120]{1,0:T(8,128)(2,1)S(1)}, u32[]{:S(2)}) %copy-start.2) | copy-done | bytes 3604504
  80.4 0.0 copy-done
  80.4 1.1 fusion.68
  81.5 0.2 reshape.684
  81.7 0.4 multiply_reduce_fusion
  82.1 0.1 copy.35
  82.2 0.0 copy-start.5
  82.3 0.0 copy-start.6
  82.3 3.6 %multiply_reduce_fusion.1 = (f32[352]{0:T(512)S(1)}, f32[352,128]{1,0:T(8,128)S(1)}) fusion(bf16[352,5120]{1,0:T(8,128)(2,1)} %copy-done.2, bf16[5120,128]{1,0:T(8,128)(2,1)} %param.13), kind=kOutput, calls=%fused_computation.49 | convolution fusion | flops 461463200 | bytes 5096832 | tf_op jit(solution)/shard_map/dot_general | solution.py:71
  85.9 0.2 fusion.16
  86.1 0.1 multiply_multiply_fusion
  86.2 0.8 multiply_cosine_fusion
  87.0 0.2 subtract_convert_fusion
  87.2 0.1 pad_maximum_fusion.3
  87.3 0.1 pad_maximum_fusion.4
  87.4 0.3 fusion.13
  87.6 0.3 fusion.60
  88.0 1.2 %fusion.63 = (f32[2,224]{1,0:T(2,128)S(1)}, f32[2,224,224]{1,2,0:T(8,128)}) fusion(pred[224,224]{0,1:T(8,128)(4,1)S(1)} %copy-done.3, bf16[352,2,64]{2,0,1:T(8,128)(2,1)S(1)} %get-tuple-element.17, bf16[352,2,64]{2,0,1:T(8,128)(2,1)S(1)} %get-tuple-element.18, bf16[352,64]{1,0:T(8,128)(2,1)S(1)} %get-tuple-element.24, ...), kind=kOutput, calls=%fused_computation.133 | convolution fusion | flops 26435808 | bytes 723712 | tf_op jit(solution)/shard_map/sub | solution.py:84
  89.1 3.5 %convolution_convert_fusion.1 = bf16[352,128]{1,0:T(8,128)(2,1)S(1)} fusion(bf16[352,5120]{1,0:T(8,128)(2,1)} %copy-done.2, bf16[5120,128]{1,0:T(8,128)(2,1)} %param.14), kind=kOutput, calls=%fused_computation.26 | convolution fusion | flops 461418496 | bytes 5005312 | tf_op jit(solution)/shard_map/dot_general | solution.py:73
  92.7 0.3 fusion.14
  93.0 0.2 fusion.15
  93.3 0.1 copy.41
  93.4 2.3 %all_gather.7 = bf16[352,512]{1,0:T(8,128)(2,1)S(1)} all-gather(bf16[352,256]{1,0:T(8,128)(2,1)S(1)} %pad_maximum_fusion.2), channel_id=1, replica_groups=mesh['groups'=2,'dp'=8,'tensor'=2] {'tensor'}, dimensions={1}, use_global_device_ids=true | all-gather | bytes 540672 | tf_op jit(solution)/shard_map/all_gather | solution.py:159
  95.7 0.0 all-to-all-done.1
  95.7 4.5 %convolution_add_fusion = bf16[352,2560]{1,0:T(8,128)(2,1)} fusion(bf16[352,512]{1,0:T(8,128)(2,1)S(1)} %all_gather.7, bf16[512,2560]{1,0:T(8,128)(2,1)} %bitcast.18, s32[]{:T(128)S(6)} %select_n.145, bf16[224,5120]{1,0:T(8,128)(2,1)} %all-gather.2.cloned.1.call-done, bf16[128,5120]{1,0:T(8,128)(2,1)} %bitcast.2), kind=kOutput, calls=%fused_computation.9 | convolution fusion | flops 928153600 | bytes 8388612 | tf_op jit(solution)/shard_map/dot_general | solution.py:170
  100.3 3.6 %gather_fusion.1 = bf16[160,2560]{1,0:T(8,128)(2,1)S(1)} fusion(bf16[352,2560]{1,0:T(8,128)(2,1)} %convolution_add_fusion, s32[1024]{0:T(1024)S(1)} %pad_clamp_fusion), kind=kCustom, calls=%fused_computation.1 | custom fusion | bytes 1639040 | tf_op jit(solution)/shard_map/jit(_take)/gather | solution.py:172
  103.9 1.3 %select_convert_fusion = bf16[160,2560]{1,0:T(8,128)(2,1)} fusion(bf16[160,2560]{1,0:T(8,128)(2,1)S(1)} %gather_fusion.1, pred[160]{0:T(512)(128)(4,1)S(1)} %get-tuple-element.13, pred[160]{0:T(512)(128)(4,1)S(1)} %fusion.58), kind=kLoop, calls=%fused_computation.15 | loop fusion | flops 819200 | bytes 1638720 | tf_op jit(solution)/shard_map/convert_element_type | solution.py:173
  (34 shorter events, 0.2 us)
Async XLA Ops:
  6.5 73.8 %copy-start = (bf16[5120,256]{1,0:T(8,128)(2,1)S(1)}, bf16[5120,256]{1,0:T(8,128)(2,1)}, u32[]{:S(2)}) copy-start(bf16[5120,256]{1,0:T(8,128)(2,1)} %param.12) | copy-start | bytes 7864324
  6.5 16.0 %all-gather.2.cloned.1.call-start = ((), (), s32[]{:S(2)}) async-start(), calls=%async_computation.2 | async-start | bytes 3440640 | tf_op jit(solution)/shard_map/all_gather | solution.py:58
  30.7 37.7 %all-to-all-start = ((bf16[8,16,5120]{2,1,0:T(8,128)(2,1)}), bf16[8,16,5120]{2,1,0:T(8,128)(2,1)}, u32[]{:S(2)}, u32[]{:S(2)}) async-start(bf16[8,16,5120]{2,1,0:T(8,128)(2,1)} %broadcast_select_fusion), calls=%async_computation | async-start | bytes 2621440 | tf_op jit(solution)/shard_map/all_to_all | solution.py:140
  68.4 27.3 %all-to-all-start.1 = ((bf16[2,256,2560]{2,1,0:T(8,128)(2,1)}), bf16[2,256,2560]{2,1,0:T(8,128)(2,1)}, u32[]{:S(2)}, u32[]{:S(2)}) async-start(bf16[2,256,2560]{2,1,0:T(8,128)(2,1)} %pad_maximum_fusion.1), calls=%async_computation.1 | async-start | bytes 5242880 | tf_op jit(solution)/shard_map/all_to_all | solution.py:163
  73.4 3.0 %copy-start.1 = (bf16[224,5120]{1,0:T(8,128)(2,1)S(1)}, bf16[224,5120]{1,0:T(8,128)(2,1)}, u32[]{:S(2)}) copy-start(bf16[224,5120]{1,0:T(8,128)(2,1)} %all-gather.2.cloned.1.call-done) | copy-start | bytes 6881284
  73.5 3.0 %copy-start.4 = (f32[5120]{0:T(1024)S(1)}, f32[5120]{0:T(1024)}, u32[]{:S(2)}) copy-start(f32[5120]{0:T(1024)} %param.11) | copy-start | bytes 61444
  78.6 1.8 %copy-start.2 = (bf16[352,5120]{1,0:T(8,128)(2,1)}, bf16[352,5120]{1,0:T(8,128)(2,1)S(1)}, u32[]{:S(2)}) copy-start(bf16[352,5120]{1,0:T(8,128)(2,1)S(1)} %fusion.4) | copy-start | bytes 10813444
  82.2 3.7 %copy-start.5 = (f32[128]{0:T(128)S(1)}, f32[128]{0:T(128)}, u32[]{:S(2)}) copy-start(f32[128]{0:T(128)} %param.16) | copy-start | bytes 1540
  82.3 3.8 %copy-start.6 = (f32[128]{0:T(128)S(1)}, f32[128]{0:T(128)}, u32[]{:S(2)}) copy-start(f32[128]{0:T(128)} %param.17) | copy-start | bytes 1540
  82.3 3.9 %copy-start.7 = (f32[64]{0:T(128)S(1)}, f32[64]{0:T(128)}, u32[]{:S(2)}) copy-start(f32[64]{0:T(128)} %multiply_power_fusion) | copy-start | bytes 772
  85.9 2.1 %copy-start.3 = (pred[224,224]{0,1:T(8,128)(4,1)S(1)}, pred[224,224]{0,1:T(8,128)(4,1)}, u32[]{:S(2)}) copy-start(pred[224,224]{0,1:T(8,128)(4,1)} %compare_and_fusion) | copy-start | bytes 150532
  89.1 3.6 %copy-start.8 = (f32[2,224,224]{1,2,0:T(8,128)S(1)}, f32[2,224,224]{1,2,0:T(8,128)}, u32[]{:S(2)}) copy-start(f32[2,224,224]{1,2,0:T(8,128)} %get-tuple-element.39) | copy-start | bytes 1204228
Sparse Core Ops, SparseCore 0:
  8.9 13.5 all-gather.1
